TPU v7x, 32 devices: a whole 2x2x4 slice. The times are simulated.
32 devices in a mesh: sec: 2 (over x), tp: 4 (over y, core), blk: 4 (over z).
Axes of the slice: x: 2, y: 2, z: 4, core: 2. Of those that a mesh axis runs over, the one named last changes fastest.
Arguments:
- perambulator: bfloat16 [4, 2, 2048, 2048], P('tp', None, 'blk'), may hold values from -0.125 to 0.125
- backward: bfloat16 [4, 2, 2048, 2048], P('tp', None, None, 'blk'), may hold values from -0.125 to 0.125
- elementals: bfloat16 [2, 4, 2, 2048, 128], P('sec', 'tp', None, 'blk'), may hold values from -6 to 6
- diagrams: int32 [4, 16, 2], P('tp'), may hold values from 0 to 3
- owner_loads: int32 [4], P('tp'), may hold values from 1 to 16, as said below
Outputs:
- hadron: float32 [2, 4, 2, 128, 128], P('sec', 'tp', None, 'blk')
Inputs may be any that keep to these rules, and one draw needn't show every extreme that they name: `diagrams`: pair indices of each owner's slots; slots at or past the owner's load are ignored. `owner_loads`: some owner has exactly 16 live slots.
All inputs are finite; a program needn't handle non-finite values.
Results may differ from a plain program's by a relative error of at most 0.007.
Values may be sent and summed in bfloat16 or wider, within the bound.
A program may use at most 64 MiB of HBM per device.

v0:
```python
import jax
import jax.numpy as jnp
from jax import lax
from jax.sharding import PartitionSpec as P


def passed_along(block, axis, distance):
    devices = range(lax.axis_size(axis))
    route = [((i - distance) % len(devices), i) for i in devices]
    return lax.ppermute(block, axis, route)


def complex_einsum(form, left_real, left_imag, right_real, right_imag, conj_left):
    if conj_left:
        real_part = jnp.einsum(
            form, left_real, right_real, preferred_element_type=jnp.float32
        ) + jnp.einsum(form, left_imag, right_imag, preferred_element_type=jnp.float32)
        imag_part = jnp.einsum(
            form, left_real, right_imag, preferred_element_type=jnp.float32
        ) - jnp.einsum(form, left_imag, right_real, preferred_element_type=jnp.float32)
    else:
        real_part = jnp.einsum(
            form, left_real, right_real, preferred_element_type=jnp.float32
        ) - jnp.einsum(form, left_imag, right_imag, preferred_element_type=jnp.float32)
        imag_part = jnp.einsum(
            form, left_real, right_imag, preferred_element_type=jnp.float32
        ) + jnp.einsum(form, left_imag, right_real, preferred_element_type=jnp.float32)
    return (real_part, imag_part)


def on_device(perambulator, backward, elementals, diagrams, owner_loads):
    tile_width = elementals.shape[4]
    full_order = perambulator.shape[3]
    source = elementals[0]
    tile_piece = lax.all_gather(elementals, "blk", axis=3, tiled=True)[0]
    real_part, imag_part = complex_einsum(
        "prc,pck->prk",
        perambulator[:, 0],
        perambulator[:, 1],
        tile_piece[:, 0],
        tile_piece[:, 1],
        False,
    )
    first_image = jnp.stack([real_part, imag_part], axis=1).astype(jnp.bfloat16)
    real_part, imag_part = complex_einsum(
        "pri,pik->rpk", backward[:, 0], backward[:, 1], first_image[:, 0], first_image[:, 1], False
    )
    dressed_elementals = lax.psum_scatter(
        jnp.stack([real_part, imag_part], axis=2), "blk", scatter_dimension=0, tiled=True
    ).astype(jnp.bfloat16)
    sink_block_tiles = passed_along(source, "sec", 1)
    norm_scale = full_order ** (-0.5)
    block_real, block_imag = complex_einsum(
        "ild,lio->ido",
        sink_block_tiles[:, 0],
        sink_block_tiles[:, 1],
        dressed_elementals[:, :, 0],
        dressed_elementals[:, :, 1],
        True,
    )
    partial_value = jnp.stack([block_real, block_imag], axis=1) * norm_scale
    owner_list = diagrams[0]
    owner_load = owner_loads[0]
    slot_count = owner_list.shape[0]
    quarter = tile_width // lax.axis_size("blk")
    share_index = lax.axis_index("blk")
    blocks = lax.psum(partial_value, "blk").astype(jnp.bfloat16)
    received_pieces = lax.all_gather(blocks, "tp", axis=0, tiled=True)
    piece_ids = jnp.arange(received_pieces.shape[0], dtype=jnp.int32)
    left_select = (owner_list[:, 0:1] == piece_ids[None, :]).astype(jnp.bfloat16)
    right_select = (owner_list[:, 1:2] == piece_ids[None, :]).astype(jnp.bfloat16)
    left_select, right_select = (left_select, right_select)
    share_rows = lax.dynamic_slice_in_dim(received_pieces, share_index * quarter, quarter, 2)
    left_addition = jnp.einsum(
        "gj,jcrk->gcrk", left_select, share_rows, preferred_element_type=jnp.float32
    )
    right_add = jnp.einsum(
        "gj,jcrk->gcrk", right_select, received_pieces, preferred_element_type=jnp.float32
    )
    left_blocks = left_addition
    right_blocks = right_add
    left_blocks = left_blocks.astype(jnp.bfloat16)
    right_blocks = right_blocks.astype(jnp.bfloat16)
    active = (jnp.arange(slot_count, dtype=jnp.int32) < owner_load).astype(jnp.bfloat16)
    masked = left_blocks * active[:, None, None, None]
    left_flat = jnp.transpose(masked, (1, 2, 0, 3)).reshape(2, quarter, slot_count * tile_width)
    right_flat = jnp.transpose(right_blocks, (1, 0, 2, 3)).reshape(
        2, slot_count * tile_width, tile_width
    )
    hadron_real, hadron_imag = complex_einsum(
        "rk,km->rm", left_flat[0], left_flat[1], right_flat[0], right_flat[1], False
    )
    total = jnp.stack([hadron_real, hadron_imag], axis=0)
    total = total * (tile_width * slot_count) ** (-0.5)
    return total.reshape(1, 1, 2, quarter, tile_width)


def solution(mesh):
    placed = (
        P("tp", None, "blk", None),
        P("tp", None, None, "blk"),
        P("sec", "tp", None, "blk", None),
        P("tp", None, None),
        P("tp"),
    )
    return jax.shard_map(
        on_device,
        mesh=mesh,
        in_specs=placed,
        out_specs=P("sec", "tp", None, "blk", None),
        check_vma=False,
    )
```

profile of v0, /device:TPU:0, one launch (start us, length us, event | category | flops | bytes accessed | tf_op | source)
XLA Modules:
  0.0 132.7 jit_solution(9880764379089832146)
XLA Ops:
  6.5 0.7 all-gather.2.cloned.1.call-update
  7.3 32.3 %all-gather.2.cloned.1.call-done = bf16[1,1,2,2048,128]{4,3,2,1,0:T(8,128)(2,1)} async-done(((bf16[1,1,2,512,128]{4,3,2,1,0:T(8,128)(2,1)}), bf16[1,1,2,2048,128]{4,3,2,1,0:T(8,128)(2,1)}) %all-gather.2.cloned.1.call-update) | async-done | bytes 1048592 | tf_op jit(solution)/shard_map/all_gather | solution.py:35
  39.6 2.5 %fusion.8 = f32[512,128]{1,0:T(8,128)S(1)} fusion(bf16[1,2,512,2048]{3,2,1,0:T(8,128)(2,1)} %param.5, bf16[1,2,2048,128]{3,2,1,0:T(8,128)(2,1)} %bitcast.137), kind=kOutput, calls=%fused_computation.11 | convolution fusion | flops 268435456 | bytes 2883584 | tf_op jit(solution)/shard_map/prc,pck->prk/dot_general | solution.py:27
  42.1 2.3 %fusion.10 = f32[512,128]{1,0:T(8,128)S(1)} fusion(bf16[1,2,512,2048]{3,2,1,0:T(8,128)(2,1)} %param.5, bf16[1,2,2048,128]{3,2,1,0:T(8,128)(2,1)S(1)} %bitcast.138), kind=kOutput, calls=%fused_computation.13 | convolution fusion | flops 268435456 | bytes 2883584 | tf_op jit(solution)/shard_map/prc,pck->prk/dot_general | solution.py:24
  44.5 0.7 fusion.33
  45.2 0.7 fusion.36
  45.9 0.7 copy-done
  46.6 0.8 fusion.4
  47.5 0.8 fusion.6
  48.3 0.8 fusion
  49.1 0.8 fusion.1
  49.9 1.5 %pad_maximum_fusion = f32[2048,1,2,128]{0,3,2,1:T(8,128)} fusion(f32[2048,1,1,128]{0,3,2,1:T(8,128)S(1)} %fusion, f32[2048,1,1,128]{0,3,2,1:T(8,128)S(1)} %fusion.1), kind=kLoop, calls=%fused_computation.4 | loop fusion | flops 524288 | bytes 4194304 | tf_op jit(solution)/shard_map/stack | solution.py:49
  51.4 0.9 copy-done.1
  52.4 1.5 %collective-permute-start = (bf16[1,2,512,128]{3,2,1,0:T(8,128)(2,1)S(1)}, bf16[1,2,512,128]{3,2,1,0:T(8,128)(2,1)S(1)}, u32[]{:S(2)}, u32[]{:S(2)}) collective-permute-start(bf16[1,2,512,128]{3,2,1,0:T(8,128)(2,1)S(1)} %bitcast.135), channel_id=1, source_target_pairs={{16,0},{0,16},{17,1},{1,17},{18,2},{2,18},{19,3},{3,19},{20,4},{4,... | collective-permute-start | bytes 786440 | tf_op jit(solution)/shard_map/ppermute | solution.py:10
  54.5 40.4 %reduce-scatter.2.cloned.1.call-done = f32[512,1,2,128]{0,3,2,1:T(8,128)} async-done(((f32[2048,1,2,128]{0,3,2,1:T(8,128)}), f32[512,1,2,128]{0,3,2,1:T(8,128)}) %reduce-scatter.2.cloned.1.call-update) | async-done | bytes 524304 | tf_op jit(solution)/shard_map/reduce_scatter | solution.py:48
  94.9 1.1 convert_element_type.36
  96.0 0.2 fusion.46
  96.2 0.2 fusion.45
  96.4 0.2 fusion.40
  96.6 0.2 fusion.39
  96.8 19.3 %all-reduce.1 = bf16[1,2,128,128]{2,3,1,0:T(8,128)(2,1)S(1)} all-reduce(f32[1,2,128,128]{2,3,1,0:T(8,128)S(1)} %maximum_multiply_fusion), channel_id=1, replica_groups=mesh['sec'=2,'tp'=4,'blk'=4] {'blk'}, use_global_device_ids=true, to_apply=%region_1.0 | all-reduce | flops 32768 | bytes 196608 | tf_op jit(solution)/shard_map/psum | solution.py:67
  116.2 5.8 %all_gather.7 = bf16[4,2,128,128]{3,2,1,0:T(8,128)(2,1)S(1)} all-gather(bf16[1,2,128,128]{3,2,1,0:T(8,128)(2,1)S(1)} %copy.16), channel_id=1, replica_groups=mesh['sec'=2,'tp'=4,'blk'=4] {'tp'}, dimensions={0}, use_global_device_ids=true | all-gather | bytes 327680 | tf_op jit(solution)/shard_map/all_gather | solution.py:68
  122.0 0.2 copy.17
  122.2 0.3 fusion.26
  122.6 0.5 copy.31
  123.1 0.5 fusion.24
  123.6 0.3 convolution_bitcast_fusion.2
  123.9 0.3 convolution_bitcast_fusion
  124.2 0.5 copy.29
  124.7 0.3 fusion.42
  125.0 0.3 fusion.44
  125.3 0.6 maximum_multiply_fusion.1
  (17 shorter events, 0.2 us)
Async XLA Ops:
  6.5 33.1 %all-gather.2.cloned.1.call-start = ((), (), s32[]{:S(2)}) async-start(), calls=%async_computation.1 | async-start | bytes 1310720 | tf_op jit(solution)/shard_map/all_gather | solution.py:35
  7.3 87.7 %reduce-scatter.2.cloned.1.call-start = ((), (), s32[]{:S(2)}) async-start(), calls=%async_computation.2 | async-start | bytes 2621440 | tf_op jit(solution)/shard_map/reduce_scatter | solution.py:48
  39.6 2.5 %copy-start.4 = (bf16[1,1,2,2048,128]{4,3,2,1,0:T(8,128)(2,1)S(1)}, bf16[1,1,2,2048,128]{4,3,2,1,0:T(8,128)(2,1)}, u32[]{:S(2)}) copy-start(bf16[1,1,2,2048,128]{4,3,2,1,0:T(8,128)(2,1)} %all-gather.2.cloned.1.call-done) | copy-start | bytes 3145732
  39.6 4.9 %copy-start.3 = (bf16[1,2,512,2048]{3,2,1,0:T(8,128)(2,1)S(1)}, bf16[1,2,512,2048]{3,2,1,0:T(8,128)(2,1)}, u32[]{:S(2)}) copy-start(bf16[1,2,512,2048]{3,2,1,0:T(8,128)(2,1)} %param.5) | copy-start | bytes 12582916
  44.5 2.2 %copy-start = (bf16[1,2,2048,512]{3,2,1,0:T(8,128)(2,1)S(1)}, bf16[1,2,2048,512]{3,2,1,0:T(8,128)(2,1)}, u32[]{:S(2)}) copy-start(bf16[1,2,2048,512]{3,2,1,0:T(8,128)(2,1)} %param.6) | copy-start | bytes 12582916
  51.4 0.9 copy-start.1
  51.4 3.1 %copy-start.2 = (s32[1,16,2]{1,2,0:T(2,128)S(1)}, s32[1,16,2]{1,2,0:T(2,128)}, u32[]{:S(2)}) copy-start(s32[1,16,2]{1,2,0:T(2,128)} %param.8) | copy-start | bytes 388
  52.4 43.7 %collective-permute-start = (bf16[1,2,512,128]{3,2,1,0:T(8,128)(2,1)S(1)}, bf16[1,2,512,128]{3,2,1,0:T(8,128)(2,1)S(1)}, u32[]{:S(2)}, u32[]{:S(2)}) collective-permute-start(bf16[1,2,512,128]{3,2,1,0:T(8,128)(2,1)S(1)} %bitcast.135), channel_id=1, source_target_pairs={{16,0},{0,16},{17,1},{1,17},{18,2},{2,18},{19,3},{3,19},{20,4},{4,... | collective-permute-start | bytes 786440 | tf_op jit(solution)/shard_map/ppermute | solution.py:10
Sparse Core Ops, SparseCore 0:
  8.9 30.6 all-gather.1
  51.6 43.3 reduce-scatter.1
where the time goes:
time: 133 us
  waiting for transfers between devices  73.4 us (55%)
  blocking collectives  25.1 us (19%)
  between operations  14.3 us (11%)
  matrix products  12.2 us (9%)
  other arithmetic  3.21 us (2%)
  local copies, waits for them, and re-layouts  2.96 us (2%)
  starting transfers between devices  1.5 us (1%)
    reduce_scatter x1, waiting for transfers between devices, on_device(): lax.psum_scatter(jnp.stack([real_part, imag_part], axis=2), 'blk', scatte...  40.4 us
    all_gather x1, waiting for transfers between devices, on_device(): tile_piece = lax.all_gather(elementals, 'blk', axis=3, tiled=True)[0]  32.3 us
    psum x1, blocking collectives, on_device(): blocks = lax.psum(partial_value, 'blk').astype(jnp.bfloat16)  19.3 us
    all_gather x1, blocking collectives, on_device(): received_pieces = lax.all_gather(blocks, 'tp', axis=0, tiled=True)  5.79 us
    dot_general x4, matrix products, complex_einsum(): jnp.einsum(form, left_imag, right_real, preferred_element_type=jnp.float32)  3.81 us
    dot_general x4, matrix products, complex_einsum(): jnp.einsum(form, left_imag, right_imag, preferred_element_type=jnp.float32)  3.57 us
  transfers between devices with their start and end apart: 3, of which 2 were waited for; matrix products, arithmetic and copies ran while one was open for 1% of the time, Pallas kernels for 0%

commit v1 on v0

v1 whole, which is shorter than its diff:
```python
import functools

import jax
import jax.numpy as jnp
from jax import lax
from jax.experimental import pallas as pl
from jax.experimental.pallas import tpu as pltpu
from jax.sharding import PartitionSpec as P

PARTS = 2
PIECES = 2
MESH = pl.DeviceIdType.MESH


def kernel(
    n_sec, n_tp, n_blk,
    tau_hbm, beta_hbm, tile_hbm, diagrams, loads, out,
    tau, beta, tile, gathered, image, conj_w, w_send, w_recv, image_full,
    partial, shares, blocks,
    load_sem, tile_sem, send_sem, recv_sem, w_send_sem, w_recv_sem,
    share_send_sem, share_recv_sem, block_send_sem, block_recv_sem,
):
    sec, tp, me = lax.axis_index("sec"), lax.axis_index("tp"), lax.axis_index("blk")
    rows, order = tau_hbm.shape[2], tau_hbm.shape[3]
    width = tile_hbm.shape[4]
    half = width // PARTS
    piece = rows // PIECES
    quarter = width // n_blk
    slots = diagrams.shape[1]

    both = jnp.minimum(me, n_blk - 1 - me)
    longer_below = me > n_blk - 1 - me

    def at_step(t):
        in_both = t <= 2 * both
        distance = jnp.where(in_both, lax.div(t + 1, 2), t - both)
        below = jnp.where(in_both, lax.rem(t, 2), jnp.where(longer_below, 1, 0))
        chunk = jnp.where(below == 1, me - distance, me + distance)
        return distance, below, chunk

    def rows_of(chunk):
        return pl.ds(pl.multiple_of(chunk * rows, rows), rows)

    def load(t):
        where = rows_of(at_step(t)[2])
        return (
            pltpu.make_async_copy(
                tau_hbm.at[0, :, :, where], tau.at[:, :, where], load_sem.at[0, t]
            ),
            pltpu.make_async_copy(
                beta_hbm.at[0, :, where, :], beta.at[:, where, :], load_sem.at[1, t]
            ),
        )

    own_tile = pltpu.make_async_copy(tile_hbm.at[0, 0], tile, tile_sem)
    own_tile.start()

    barrier = pltpu.get_barrier_semaphore()
    peers = n_tp * n_blk

    def greet(k, _):
        other_tp, other_blk = lax.div(k, n_blk), lax.rem(k, n_blk)

        @pl.when(jnp.logical_or(other_tp != tp, other_blk != me))
        def _():
            pl.semaphore_signal(
                barrier, inc=1, device_id=(sec, other_tp, other_blk), device_id_type=MESH
            )

        return 0

    lax.fori_loop(0, peers, greet, 0)
    sec_next = lax.rem(sec + 1, n_sec)
    sec_back = lax.rem(sec + n_sec - 1, n_sec)
    greeted = peers - 1
    if n_sec > 1:
        pl.semaphore_signal(barrier, inc=1, device_id=(sec_next, tp, me), device_id_type=MESH)
        greeted += 1
    if n_sec > 2:
        pl.semaphore_signal(barrier, inc=1, device_id=(sec_back, tp, me), device_id_type=MESH)
        greeted += 1

    for t in range(n_blk):
        for copy in load(t):
            copy.start()

    own_tile.wait()
    lane = lax.broadcasted_iota(jnp.int32, (rows, width), 1)
    real = tile[0].astype(jnp.float32)
    imag = tile[1].astype(jnp.float32)
    gathered[0, rows_of(me), :] = jnp.where(
        lane < half, real, pltpu.roll(imag, half, 1)
    ).astype(jnp.bfloat16)
    gathered[1, rows_of(me), :] = jnp.where(
        lane < half, pltpu.roll(real, half, 1), imag
    ).astype(jnp.bfloat16)
    image[...] = jnp.zeros_like(image)
    conj_w[...] = jnp.zeros_like(conj_w)
    pl.semaphore_wait(barrier, greeted)

    def pass_on(upward, distance, part, r):
        chunk = jnp.where(upward == 1, me - distance, me + distance)
        target = jnp.where(upward == 1, me + 1, me - 1)
        where = pl.ds(pl.multiple_of(chunk * rows + r * piece, piece), piece)
        block = gathered.at[part, where, :]
        return pltpu.make_async_remote_copy(
            src_ref=block,
            dst_ref=block,
            send_sem=send_sem.at[upward, distance, part, r],
            recv_sem=recv_sem.at[upward, distance, part, r],
            device_id=(sec, tp, target),
            device_id_type=MESH,
        )

    def arrival(below, distance, part, r):
        chunk = jnp.where(below == 1, me - distance, me + distance)
        where = pl.ds(pl.multiple_of(chunk * rows + r * piece, piece), piece)
        block = gathered.at[part, where, :]
        return pltpu.make_async_remote_copy(
            src_ref=block,
            dst_ref=block,
            send_sem=send_sem.at[below, distance, part, r],
            recv_sem=recv_sem.at[below, distance - 1, part, r],
            device_id=(sec, tp, me),
            device_id_type=MESH,
        )

    def send_own(upward, part):
        for r in range(PIECES):
            pass_on(upward, 0, part, r).start()

    @pl.when(me < n_blk - 1)
    def _():
        send_own(1, 0)

    @pl.when(me > 0)
    def _():
        send_own(0, 0)

    for part in range(1, PARTS):
        @pl.when(me == 0)
        def _():
            send_own(1, part)

        @pl.when(me == n_blk - 1)
        def _():
            send_own(0, part)

    def w_copy(part):
        return pltpu.make_async_remote_copy(
            src_ref=w_send.at[part],
            dst_ref=w_recv.at[part],
            send_sem=w_send_sem.at[part],
            recv_sem=w_recv_sem.at[part],
            device_id=(sec_next, tp, me),
            device_id_type=MESH,
        )

    piece_lane = lax.broadcasted_iota(jnp.int32, (piece, width), 1)
    for part in range(PARTS):
        def step(u, _):
            t, r = lax.div(u, PIECES), lax.rem(u, PIECES)
            distance, below, chunk = at_step(t)

            @pl.when(t > 0)
            def _():
                arrival(below, distance, part, r).wait_recv()
                more = jnp.where(below == 1, me < n_blk - 1, me > 0)

                @pl.when(more)
                def _():
                    pass_on(below, distance, part, r).start()
                    if part + 1 < PARTS:
                        last = jnp.where(below == 1, chunk == 0, chunk == n_blk - 1)

                        @pl.when(jnp.logical_and(last, r == PIECES - 1))
                        def _():
                            send_own(below, part + 1)

            if part == 0:
                @pl.when(r == 0)
                def _():
                    for copy in load(t):
                        copy.wait()

            where = pl.ds(pl.multiple_of(chunk * rows + r * piece, piece), piece)
            straight = gathered[part, where, :]
            wide = straight.astype(jnp.float32)
            turned = pltpu.roll(wide, half, 1)
            turned = jnp.where(piece_lane < half, -turned, turned)
            crossed = turned.astype(jnp.bfloat16)
            image[part] += jnp.dot(
                tau[0, :, where], straight, preferred_element_type=jnp.float32
            ) + jnp.dot(tau[1, :, where], crossed, preferred_element_type=jnp.float32)
            conj_w[part] += jnp.dot(
                wide.T.astype(jnp.bfloat16),
                beta[0, where, :],
                preferred_element_type=jnp.float32,
            ) + jnp.dot(
                (-turned).T.astype(jnp.bfloat16),
                beta[1, where, :],
                preferred_element_type=jnp.float32,
            )
            return 0

        lax.fori_loop(0, n_blk * PIECES, step, 0)
        if n_sec > 1:
            w_send[part] = conj_w[part].astype(jnp.bfloat16)
            w_copy(part).start()
        else:
            w_recv[part] = conj_w[part].astype(jnp.bfloat16)

    first, second = image[0], image[1]
    image_full[:, :width] = jnp.where(
        lane < half, first, pltpu.roll(second, half, 1)
    ).astype(jnp.bfloat16)
    image_full[:, width:] = jnp.where(
        lane < half, pltpu.roll(first, half, 1), second
    ).astype(jnp.bfloat16)

    for part in range(PARTS):
        if n_sec > 1:
            w_copy(part).wait_recv()
        product = jnp.dot(w_recv[part], image_full[...], preferred_element_type=jnp.float32)
        own = pl.ds(part * half, half)
        partial[0, own, :] = (product[:half, :width] + product[half:, width:]).astype(jnp.bfloat16)
        partial[1, own, :] = (product[:half, width:] - product[half:, :width]).astype(jnp.bfloat16)

    def rows_share(q):
        return partial.at[:, pl.ds(pl.multiple_of(q * quarter, quarter), quarter), :]

    def share_copy(distance):
        target = lax.rem(me + distance, n_blk)
        return pltpu.make_async_remote_copy(
            src_ref=rows_share(target),
            dst_ref=shares.at[distance - 1],
            send_sem=share_send_sem.at[distance - 1],
            recv_sem=share_recv_sem.at[distance - 1],
            device_id=(sec, tp, target),
            device_id_type=MESH,
        )

    for distance in range(1, n_blk):
        share_copy(distance).start()
    total = partial[:, pl.ds(pl.multiple_of(me * quarter, quarter), quarter), :].astype(jnp.float32)
    for distance in range(1, n_blk):
        share_copy(distance).wait_recv()
        total = total + shares[distance - 1].astype(jnp.float32)
    blocks[tp, me] = (total * order ** (-0.5)).astype(jnp.bfloat16)

    def block_copy(k, sending):
        other_tp, other_blk = lax.div(k, n_blk), lax.rem(k, n_blk)
        if sending:
            slot, sem = blocks.at[tp, me], block_recv_sem.at[tp, me]
        else:
            slot, sem = blocks.at[other_tp, other_blk], block_recv_sem.at[other_tp, other_blk]
        copy = pltpu.make_async_remote_copy(
            src_ref=slot,
            dst_ref=slot,
            send_sem=block_send_sem.at[other_tp, other_blk],
            recv_sem=sem,
            device_id=(sec, other_tp, other_blk),
            device_id_type=MESH,
        )
        return copy, jnp.logical_or(other_tp != tp, other_blk != me)

    def start_block(k, _):
        copy, other = block_copy(k, True)

        @pl.when(other)
        def _():
            copy.start()

        return 0

    def wait_block(k, _):
        copy, other = block_copy(k, False)

        @pl.when(other)
        def _():
            copy.wait_recv()

        return 0

    lax.fori_loop(0, peers, start_block, 0)
    lax.fori_loop(0, peers, wait_block, 0)

    sums = jnp.zeros((2 * quarter, 2 * width), jnp.float32)
    for g in range(slots):
        active = jnp.where(g < loads[0], 1.0, 0.0)
        left = blocks[diagrams[0, g, 0], me].reshape(2 * quarter, width)
        left = (left.astype(jnp.float32) * active).astype(jnp.bfloat16)
        right = blocks[diagrams[0, g, 1]]
        right = jnp.concatenate(
            [right[:, 0].reshape(width, width), right[:, 1].reshape(width, width)], axis=1
        )
        sums = sums + jnp.dot(left, right, preferred_element_type=jnp.float32)
    scale = (width * slots) ** (-0.5)
    out[0, 0, 0] = (sums[:quarter, :width] - sums[quarter:, width:]) * scale
    out[0, 0, 1] = (sums[:quarter, width:] + sums[quarter:, :width]) * scale

    def drain(u, _):
        distance = lax.div(u, PIECES)
        r = lax.rem(u, PIECES)
        for part in range(PARTS):
            @pl.when(jnp.logical_and(distance <= me, me < n_blk - 1))
            def _():
                pass_on(1, distance, part, r).wait_send()

            @pl.when(jnp.logical_and(me + distance < n_blk, me > 0))
            def _():
                pass_on(0, distance, part, r).wait_send()

        return 0

    lax.fori_loop(0, n_blk * PIECES, drain, 0)
    if n_sec > 1:
        for part in range(PARTS):
            w_copy(part).wait_send()
    for distance in range(1, n_blk):
        share_copy(distance).wait_send()

    def drain_block(k, _):
        copy, other = block_copy(k, True)

        @pl.when(other)
        def _():
            copy.wait_send()

        return 0

    lax.fori_loop(0, peers, drain_block, 0)


def on_device(n_sec, n_tp, n_blk, perambulator, backward, elementals, diagrams, owner_loads):
    rows, order = perambulator.shape[2:]
    width = elementals.shape[4]
    half = width // PARTS
    quarter = width // n_blk
    any_space = pl.BlockSpec(memory_space=pl.ANY)
    smem = pl.BlockSpec(memory_space=pltpu.SMEM)
    dma = pltpu.SemaphoreType.DMA
    return pl.pallas_call(
        functools.partial(kernel, n_sec, n_tp, n_blk),
        out_shape=jax.ShapeDtypeStruct((1, 1, 2, quarter, width), jnp.float32),
        in_specs=[any_space, any_space, any_space, smem, smem],
        out_specs=pl.BlockSpec(memory_space=pltpu.VMEM),
        scratch_shapes=[
            pltpu.VMEM((2, rows, order), jnp.bfloat16),
            pltpu.VMEM((2, order, rows), jnp.bfloat16),
            pltpu.VMEM((2, rows, width), jnp.bfloat16),
            pltpu.VMEM((PARTS, order, 2 * half), jnp.bfloat16),
            pltpu.VMEM((PARTS, rows, 2 * half), jnp.float32),
            pltpu.VMEM((PARTS, 2 * half, rows), jnp.float32),
            pltpu.VMEM((PARTS, 2 * half, rows), jnp.bfloat16),
            pltpu.VMEM((PARTS, 2 * half, rows), jnp.bfloat16),
            pltpu.VMEM((rows, 2 * width), jnp.bfloat16),
            pltpu.VMEM((2, width, width), jnp.bfloat16),
            pltpu.VMEM((n_blk, 2, quarter, width), jnp.bfloat16),
            pltpu.VMEM((n_tp, n_blk, 2, quarter, width), jnp.bfloat16),
            dma((2, n_blk)),
            dma,
            dma((2, n_blk, PARTS, PIECES)),
            dma((2, n_blk, PARTS, PIECES)),
            dma((PARTS,)),
            dma((PARTS,)),
            dma((n_blk,)),
            dma((n_blk,)),
            dma((n_tp, n_blk)),
            dma((n_tp, n_blk)),
        ],
        compiler_params=pltpu.CompilerParams(
            collective_id=0, has_side_effects=True, vmem_limit_bytes=40 * 1024 * 1024
        ),
    )(perambulator, backward, elementals, diagrams, owner_loads)


def solution(mesh):
    placed = (
        P("tp", None, "blk", None),
        P("tp", None, None, "blk"),
        P("sec", "tp", None, "blk", None),
        P("tp", None, None),
        P("tp"),
    )
    sizes = (mesh.shape["sec"], mesh.shape["tp"], mesh.shape["blk"])
    return jax.shard_map(
        functools.partial(on_device, *sizes),
        mesh=mesh,
        in_specs=placed,
        out_specs=P("sec", "tp", None, "blk", None),
        check_vma=False,
    )
```

time: 133 us -> 50.8 us (0.38)
  waiting for transfers between devices: 73.4 us -> 0 us
  Pallas kernels: 0 us -> 43.2 us
  blocking collectives: 25.1 us -> 0 us
  between operations: 14.3 us -> 0.66 us
  matrix products: 12.2 us -> 0 us
  local copies, waits for them, and re-layouts: 2.96 us -> 6.7 us
  other arithmetic: 3.21 us -> 0 us
  starting transfers between devices: 1.5 us -> 0 us
    pallas_call x0 -> x1, Pallas kernels: none -> 43.2 us  [on_device(): pl.pallas_call(functools.partial(kernel, n_sec, n_tp, n_blk), out_shape=j...]
    reduce_scatter x1 -> x0, waiting for transfers between devices: 40.4 us -> none  [on_device(): lax.psum_scatter(jnp.stack([real_part, imag_part], axis=2), 'blk', scatte...]
    all_gather x1 -> x0, waiting for transfers between devices: 32.3 us -> none  [on_device(): tile_piece = lax.all_gather(elementals, 'blk', axis=3, tiled=True)[0]]
    psum x1 -> x0, blocking collectives: 19.3 us -> none  [on_device(): blocks = lax.psum(partial_value, 'blk').astype(jnp.bfloat16)]
    dot_general x18 -> x0, matrix products: 12.2 us -> none  [the longest x4 3.81 us: complex_einsum(): jnp.einsum(form, left_imag, right_real, preferred_element_type=jnp.float32)]
    all_gather x1 -> x0, blocking collectives: 5.79 us -> none  [on_device(): received_pieces = lax.all_gather(blocks, 'tp', axis=0, tiled=True)]
    unnamed x10 -> x8, local copies, waits for them, and re-layouts: 1.66 us -> 6.7 us
    another operation x1 -> x0, other arithmetic: 1.49 us -> none  [on_device(): jnp.stack([real_part, imag_part], axis=2)]
  transfers between devices with their start and end apart: 3 -> 0, of which waited for: 2 -> 0; matrix products, arithmetic and copies ran while one was open for 1% -> 0% of each run, Pallas kernels for 0% -> 0%
where the time goes in v1:
time: 50.8 us; the launch traced here: 50.5 us
  Pallas kernels  43.2 us (85%)
  local copies, waits for them, and re-layouts  6.7 us (13%)
  between operations  0.66 us (1%)
    pallas_call x1, Pallas kernels, on_device(): pl.pallas_call(functools.partial(kernel, n_sec, n_tp, n_blk), out_shape=j...  43.2 us
    unnamed x8, local copies, waits for them, and re-layouts  6.7 us

profile of v1, /device:TPU:0, one launch (start us, length us, event | category | flops | bytes accessed | tf_op | source)
XLA Modules:
  0.0 50.5 jit_solution(9529395411192842066)
XLA Ops:
  0.7 0.8 %copy.6.diagrams = s32[1,16,2]{2,1,0:T(8,128)S(1)} copy(s32[1,16,2]{1,2,0:T(2,128)} %param.8) | data formatting | bytes 256 | tf_op args[3]
  1.4 0.0 copy-start
  1.4 2.2 %copy-done = bf16[1,2,512,2048]{3,2,1,0:T(8,128)(2,1)S(1)} copy-done((bf16[1,2,512,2048]{3,2,1,0:T(8,128)(2,1)S(1)}, bf16[1,2,512,2048]{3,2,1,0:T(8,128)(2,1)}, u32[]{:S(2)}) %copy-start) | copy-done | bytes 4194328
  3.6 0.0 copy-start.1
  3.6 2.2 %copy-done.1 = bf16[1,2,2048,512]{3,2,1,0:T(8,128)(2,1)S(1)} copy-done((bf16[1,2,2048,512]{3,2,1,0:T(8,128)(2,1)S(1)}, bf16[1,2,2048,512]{3,2,1,0:T(8,128)(2,1)}, u32[]{:S(2)}) %copy-start.1) | copy-done | bytes 4194328
  5.8 0.0 copy-start.2
  5.8 0.9 %copy-done.2 = bf16[1,1,2,512,128]{4,3,2,1,0:T(8,128)(2,1)S(1)} copy-done((bf16[1,1,2,512,128]{4,3,2,1,0:T(8,128)(2,1)S(1)}, bf16[1,1,2,512,128]{4,3,2,1,0:T(8,128)(2,1)}, u32[]{:S(2)}) %copy-start.2) | copy-done | bytes 262168
  6.7 43.2 %shard_map.55 = f32[1,1,2,32,128]{4,3,2,1,0:T(8,128)S(1)} custom-call(bf16[1,2,512,2048]{3,2,1,0:T(8,128)(2,1)S(1)} %copy-done, bf16[1,2,2048,512]{3,2,1,0:T(8,128)(2,1)S(1)} %copy-done.1, bf16[1,1,2,512,128]{4,3,2,1,0:T(8,128)(2,1)S(1)} %copy-done.2, s32[1,16,2]{2,1,0:T(8,128)S(1)} %copy.6.diagrams, s32[1]{0:T(128)S(6)} %copy.8.loads), custom_call_target="tpu_custom_call" | custom-call | tf_op jit(solution)/shard_map/pallas_call | solution.py:343
  49.9 0.6 %copy.9 = f32[1,1,2,32,128]{4,3,2,1,0:T(8,128)} copy(f32[1,1,2,32,128]{4,3,2,1,0:T(8,128)S(1)} %shard_map.55) | data formatting | bytes 65536
Async XLA Ops:
  1.4 2.2 %copy-start = (bf16[1,2,512,2048]{3,2,1,0:T(8,128)(2,1)S(1)}, bf16[1,2,512,2048]{3,2,1,0:T(8,128)(2,1)}, u32[]{:S(2)}) copy-start(bf16[1,2,512,2048]{3,2,1,0:T(8,128)(2,1)} %tau_hbm.1) | copy-start | bytes 12582916
  3.6 2.2 %copy-start.1 = (bf16[1,2,2048,512]{3,2,1,0:T(8,128)(2,1)S(1)}, bf16[1,2,2048,512]{3,2,1,0:T(8,128)(2,1)}, u32[]{:S(2)}) copy-start(bf16[1,2,2048,512]{3,2,1,0:T(8,128)(2,1)} %beta_hbm.1) | copy-start | bytes 12582916
  5.8 0.9 %copy-start.2 = (bf16[1,1,2,512,128]{4,3,2,1,0:T(8,128)(2,1)S(1)}, bf16[1,1,2,512,128]{4,3,2,1,0:T(8,128)(2,1)}, u32[]{:S(2)}) copy-start(bf16[1,1,2,512,128]{4,3,2,1,0:T(8,128)(2,1)} %tile_hbm.1) | copy-start | bytes 786436

commit v2 on v1

--- a/solution.py
+++ b/solution.py
@@ -26,7 +26,7 @@
     half = width // PARTS
     piece = rows // PIECES
     quarter = width // n_blk
-    slots = diagrams.shape[1]
+    slots = diagrams.shape[2]
 
     both = jnp.minimum(me, n_blk - 1 - me)
     longer_below = me > n_blk - 1 - me
@@ -288,9 +288,9 @@
     sums = jnp.zeros((2 * quarter, 2 * width), jnp.float32)
     for g in range(slots):
         active = jnp.where(g < loads[0], 1.0, 0.0)
-        left = blocks[diagrams[0, g, 0], me].reshape(2 * quarter, width)
+        left = blocks[diagrams[0, 0, g], me].reshape(2 * quarter, width)
         left = (left.astype(jnp.float32) * active).astype(jnp.bfloat16)
-        right = blocks[diagrams[0, g, 1]]
+        right = blocks[diagrams[0, 1, g]]
         right = jnp.concatenate(
             [right[:, 0].reshape(width, width), right[:, 1].reshape(width, width)], axis=1
         )
@@ -337,13 +337,13 @@
     width = elementals.shape[4]
     half = width // PARTS
     quarter = width // n_blk
-    any_space = pl.BlockSpec(memory_space=pl.ANY)
+    hbm = pl.BlockSpec(memory_space=pltpu.HBM)
     smem = pl.BlockSpec(memory_space=pltpu.SMEM)
     dma = pltpu.SemaphoreType.DMA
     return pl.pallas_call(
         functools.partial(kernel, n_sec, n_tp, n_blk),
         out_shape=jax.ShapeDtypeStruct((1, 1, 2, quarter, width), jnp.float32),
-        in_specs=[any_space, any_space, any_space, smem, smem],
+        in_specs=[hbm, hbm, hbm, smem, smem],
         out_specs=pl.BlockSpec(memory_space=pltpu.VMEM),
         scratch_shapes=[
             pltpu.VMEM((2, rows, order), jnp.bfloat16),
@@ -372,7 +372,7 @@
         compiler_params=pltpu.CompilerParams(
             collective_id=0, has_side_effects=True, vmem_limit_bytes=40 * 1024 * 1024
         ),
-    )(perambulator, backward, elementals, diagrams, owner_loads)
+    )(perambulator, backward, elementals, jnp.swapaxes(diagrams, 1, 2), owner_loads)
 
 
 def solution(mesh):

time: 50.8 us -> 50.6 us (level)
    unnamed x8 -> x9, local copies, waits for them, and re-layouts: 6.7 us -> 6.61 us
where the time goes in v2:
time: 50.6 us; the launch traced here: 50.3 us
  Pallas kernels  43.1 us (85%)
  local copies, waits for them, and re-layouts  6.61 us (13%)
  between operations  0.67 us (1%)
    pallas_call x1, Pallas kernels, on_device(): pl.pallas_call(functools.partial(kernel, n_sec, n_tp, n_blk), out_shape=j...  43.1 us
    unnamed x9, local copies, waits for them, and re-layouts  6.61 us

profile of v2, /device:TPU:0, one launch (start us, length us, event | category | flops | bytes accessed | tf_op | source)
XLA Modules:
  0.0 50.3 jit_solution(4339269738973830152)
XLA Ops:
  0.7 0.0 copy-start
  0.7 2.2 %copy-done = bf16[1,2,512,2048]{3,2,1,0:T(8,128)(2,1)S(1)} copy-done((bf16[1,2,512,2048]{3,2,1,0:T(8,128)(2,1)S(1)}, bf16[1,2,512,2048]{3,2,1,0:T(8,128)(2,1)}, u32[]{:S(2)}) %copy-start) | copy-done | bytes 4194328
  2.8 0.0 copy-start.1
  2.8 2.2 %copy-done.1 = bf16[1,2,2048,512]{3,2,1,0:T(8,128)(2,1)S(1)} copy-done((bf16[1,2,2048,512]{3,2,1,0:T(8,128)(2,1)S(1)}, bf16[1,2,2048,512]{3,2,1,0:T(8,128)(2,1)}, u32[]{:S(2)}) %copy-start.1) | copy-done | bytes 4194328
  5.0 0.0 copy-start.2
  5.0 0.9 %copy-done.2 = bf16[1,1,2,512,128]{4,3,2,1,0:T(8,128)(2,1)S(1)} copy-done((bf16[1,1,2,512,128]{4,3,2,1,0:T(8,128)(2,1)S(1)}, bf16[1,1,2,512,128]{4,3,2,1,0:T(8,128)(2,1)}, u32[]{:S(2)}) %copy-start.2) | copy-done | bytes 262168
  6.0 0.0 copy-start.3
  6.0 0.7 %copy-done.3 = s32[1,16,2]{1,2,0:T(2,128)S(1)} copy-done((s32[1,16,2]{1,2,0:T(2,128)S(1)}, s32[1,16,2]{1,2,0:T(2,128)}, u32[]{:S(2)}) %copy-start.3) | copy-done | bytes 152
  6.7 43.1 %shard_map.55 = f32[1,1,2,32,128]{4,3,2,1,0:T(8,128)S(1)} custom-call(bf16[1,2,512,2048]{3,2,1,0:T(8,128)(2,1)S(1)} %copy-done, bf16[1,2,2048,512]{3,2,1,0:T(8,128)(2,1)S(1)} %copy-done.1, bf16[1,1,2,512,128]{4,3,2,1,0:T(8,128)(2,1)S(1)} %copy-done.2, s32[1,2,16]{2,1,0:T(2,128)S(1)} %bitcast.1, s32[1]{0:T(128)S(6)} %copy.7.loads), custom_call_target="tpu_custom_call" | custom-call | tf_op jit(solution)/shard_map/pallas_call | solution.py:343
  49.7 0.6 %copy.8 = f32[1,1,2,32,128]{4,3,2,1,0:T(8,128)} copy(f32[1,1,2,32,128]{4,3,2,1,0:T(8,128)S(1)} %shard_map.55) | data formatting | bytes 65536
Async XLA Ops:
  0.7 2.2 %copy-start = (bf16[1,2,512,2048]{3,2,1,0:T(8,128)(2,1)S(1)}, bf16[1,2,512,2048]{3,2,1,0:T(8,128)(2,1)}, u32[]{:S(2)}) copy-start(bf16[1,2,512,2048]{3,2,1,0:T(8,128)(2,1)} %tau_hbm.1) | copy-start | bytes 12582916
  2.8 2.2 %copy-start.1 = (bf16[1,2,2048,512]{3,2,1,0:T(8,128)(2,1)S(1)}, bf16[1,2,2048,512]{3,2,1,0:T(8,128)(2,1)}, u32[]{:S(2)}) copy-start(bf16[1,2,2048,512]{3,2,1,0:T(8,128)(2,1)} %beta_hbm.1) | copy-start | bytes 12582916
  5.0 0.9 %copy-start.2 = (bf16[1,1,2,512,128]{4,3,2,1,0:T(8,128)(2,1)S(1)}, bf16[1,1,2,512,128]{4,3,2,1,0:T(8,128)(2,1)}, u32[]{:S(2)}) copy-start(bf16[1,1,2,512,128]{4,3,2,1,0:T(8,128)(2,1)} %tile_hbm.1) | copy-start | bytes 786436
  6.0 0.7 %copy-start.3 = (s32[1,16,2]{1,2,0:T(2,128)S(1)}, s32[1,16,2]{1,2,0:T(2,128)}, u32[]{:S(2)}) copy-start(s32[1,16,2]{1,2,0:T(2,128)} %param.8) | copy-start | bytes 388

commit v3 on v2

--- a/solution.py
+++ b/solution.py
@@ -18,7 +18,7 @@
     tau, beta, tile, gathered, image, conj_w, w_send, w_recv, image_full,
     partial, shares, blocks,
     load_sem, tile_sem, send_sem, recv_sem, w_send_sem, w_recv_sem,
-    share_send_sem, share_recv_sem, block_send_sem, block_recv_sem,
+    share_send_sem, share_recv_sem, block_send_sem, block_recv_sem, pair_send_sem,
 ):
     sec, tp, me = lax.axis_index("sec"), lax.axis_index("tp"), lax.axis_index("blk")
     rows, order = tau_hbm.shape[2], tau_hbm.shape[3]
@@ -58,10 +58,18 @@
     barrier = pltpu.get_barrier_semaphore()
     peers = n_tp * n_blk
 
+    cores = 2 if n_tp % 2 == 0 else 1
+    core = lax.rem(tp, cores)
+    sibling = tp + 1 - 2 * core
+
+    def same_core(other_tp, other_blk):
+        other = jnp.logical_or(other_tp != tp, other_blk != me)
+        return jnp.logical_and(other, lax.rem(other_tp, cores) == core)
+
     def greet(k, _):
         other_tp, other_blk = lax.div(k, n_blk), lax.rem(k, n_blk)
 
-        @pl.when(jnp.logical_or(other_tp != tp, other_blk != me))
+        @pl.when(same_core(other_tp, other_blk))
         def _():
             pl.semaphore_signal(
                 barrier, inc=1, device_id=(sec, other_tp, other_blk), device_id_type=MESH
@@ -72,7 +80,10 @@
     lax.fori_loop(0, peers, greet, 0)
     sec_next = lax.rem(sec + 1, n_sec)
     sec_back = lax.rem(sec + n_sec - 1, n_sec)
-    greeted = peers - 1
+    greeted = peers // cores - 1
+    if cores > 1:
+        pl.semaphore_signal(barrier, inc=1, device_id=(sec, sibling, me), device_id_type=MESH)
+        greeted += 1
     if n_sec > 1:
         pl.semaphore_signal(barrier, inc=1, device_id=(sec_next, tp, me), device_id_type=MESH)
         greeted += 1
@@ -95,6 +106,16 @@
         lane < half, pltpu.roll(real, half, 1), imag
     ).astype(jnp.bfloat16)
     image[...] = jnp.zeros_like(image)
+    dense = n_tp * n_tp <= slots
+    if dense:
+        counts = [[jnp.float32(0)] * n_tp for _ in range(n_tp)]
+        for g in range(slots):
+            left, right = diagrams[0, 0, g], diagrams[0, 1, g]
+            live = g < loads[0]
+            for a in range(n_tp):
+                in_a = jnp.where(jnp.logical_and(live, left == a), 1.0, 0.0)
+                for b in range(n_tp):
+                    counts[a][b] = counts[a][b] + jnp.where(right == b, in_a, 0.0)
     conj_w[...] = jnp.zeros_like(conj_w)
     pl.semaphore_wait(barrier, greeted)
 
@@ -158,11 +179,11 @@
 
     piece_lane = lax.broadcasted_iota(jnp.int32, (piece, width), 1)
     for part in range(PARTS):
-        def step(u, _):
+        def receive(u):
             t, r = lax.div(u, PIECES), lax.rem(u, PIECES)
             distance, below, chunk = at_step(t)
 
-            @pl.when(t > 0)
+            @pl.when(jnp.logical_and(t > 0, u < n_blk * PIECES))
             def _():
                 arrival(below, distance, part, r).wait_recv()
                 more = jnp.where(below == 1, me < n_blk - 1, me > 0)
@@ -176,6 +197,14 @@
                         @pl.when(jnp.logical_and(last, r == PIECES - 1))
                         def _():
                             send_own(below, part + 1)
+
+        def step(u, _):
+            t, r = lax.div(u, PIECES), lax.rem(u, PIECES)
+            chunk = at_step(t)[2]
+
+            @pl.when(both > 0)
+            def _():
+                receive(u + 1)
 
             if part == 0:
                 @pl.when(r == 0)
@@ -201,6 +230,11 @@
                 beta[1, where, :],
                 preferred_element_type=jnp.float32,
             )
+
+            @pl.when(both == 0)
+            def _():
+                receive(u + 1)
+
             return 0
 
         lax.fori_loop(0, n_blk * PIECES, step, 0)
@@ -242,90 +276,140 @@
 
     for distance in range(1, n_blk):
         share_copy(distance).start()
+
+    def drain(u, _):
+        distance = lax.div(u, PIECES)
+        r = lax.rem(u, PIECES)
+        for part in range(PARTS):
+            @pl.when(jnp.logical_and(distance <= me, me < n_blk - 1))
+            def _():
+                pass_on(1, distance, part, r).wait_send()
+
+            @pl.when(jnp.logical_and(me + distance < n_blk, me > 0))
+            def _():
+                pass_on(0, distance, part, r).wait_send()
+
+        return 0
+
+    lax.fori_loop(0, n_blk * PIECES, drain, 0)
     total = partial[:, pl.ds(pl.multiple_of(me * quarter, quarter), quarter), :].astype(jnp.float32)
     for distance in range(1, n_blk):
         share_copy(distance).wait_recv()
         total = total + shares[distance - 1].astype(jnp.float32)
     blocks[tp, me] = (total * order ** (-0.5)).astype(jnp.bfloat16)
 
-    def block_copy(k, sending):
-        other_tp, other_blk = lax.div(k, n_blk), lax.rem(k, n_blk)
-        if sending:
-            slot, sem = blocks.at[tp, me], block_recv_sem.at[tp, me]
-        else:
-            slot, sem = blocks.at[other_tp, other_blk], block_recv_sem.at[other_tp, other_blk]
-        copy = pltpu.make_async_remote_copy(
+    def block_copy(from_tp, from_blk, to_tp, to_blk, sem):
+        slot = blocks.at[from_tp, from_blk]
+        return pltpu.make_async_remote_copy(
             src_ref=slot,
             dst_ref=slot,
-            send_sem=block_send_sem.at[other_tp, other_blk],
-            recv_sem=sem,
-            device_id=(sec, other_tp, other_blk),
+            send_sem=sem,
+            recv_sem=block_recv_sem.at[from_tp, from_blk],
+            device_id=(sec, to_tp, to_blk),
             device_id_type=MESH,
         )
-        return copy, jnp.logical_or(other_tp != tp, other_blk != me)
+
+    def own_block(k):
+        other_tp, other_blk = lax.div(k, n_blk), lax.rem(k, n_blk)
+        copy = block_copy(tp, me, other_tp, other_blk, block_send_sem.at[other_tp, other_blk])
+        return copy, same_core(other_tp, other_blk)
+
+    def sibling_block(k):
+        from_tp, from_blk = lax.div(k, n_blk), lax.rem(k, n_blk)
+        copy = block_copy(from_tp, from_blk, sibling, me, pair_send_sem.at[from_tp, from_blk])
+        return copy, lax.rem(from_tp, cores) == core
 
     def start_block(k, _):
-        copy, other = block_copy(k, True)
-
-        @pl.when(other)
+        copy, wanted = own_block(k)
+
+        @pl.when(wanted)
         def _():
             copy.start()
 
         return 0
 
     def wait_block(k, _):
-        copy, other = block_copy(k, False)
-
-        @pl.when(other)
+        other_tp, other_blk = lax.div(k, n_blk), lax.rem(k, n_blk)
+
+        @pl.when(same_core(other_tp, other_blk))
+        def _():
+            block_copy(
+                other_tp, other_blk, tp, me, block_send_sem.at[other_tp, other_blk]
+            ).wait_recv()
+            if cores > 1:
+                sibling_block(k)[0].start()
+
+        return 0
+
+    def wait_pair(k, _):
+        copy, passed = sibling_block(k)
+
+        @pl.when(jnp.logical_not(passed))
         def _():
             copy.wait_recv()
 
         return 0
 
     lax.fori_loop(0, peers, start_block, 0)
-    lax.fori_loop(0, peers, wait_block, 0)
-
-    sums = jnp.zeros((2 * quarter, 2 * width), jnp.float32)
-    for g in range(slots):
-        active = jnp.where(g < loads[0], 1.0, 0.0)
-        left = blocks[diagrams[0, 0, g], me].reshape(2 * quarter, width)
-        left = (left.astype(jnp.float32) * active).astype(jnp.bfloat16)
-        right = blocks[diagrams[0, 1, g]]
-        right = jnp.concatenate(
-            [right[:, 0].reshape(width, width), right[:, 1].reshape(width, width)], axis=1
-        )
-        sums = sums + jnp.dot(left, right, preferred_element_type=jnp.float32)
-    scale = (width * slots) ** (-0.5)
-    out[0, 0, 0] = (sums[:quarter, :width] - sums[quarter:, width:]) * scale
-    out[0, 0, 1] = (sums[:quarter, width:] + sums[quarter:, :width]) * scale
-
-    def drain(u, _):
-        distance = lax.div(u, PIECES)
-        r = lax.rem(u, PIECES)
-        for part in range(PARTS):
-            @pl.when(jnp.logical_and(distance <= me, me < n_blk - 1))
-            def _():
-                pass_on(1, distance, part, r).wait_send()
-
-            @pl.when(jnp.logical_and(me + distance < n_blk, me > 0))
-            def _():
-                pass_on(0, distance, part, r).wait_send()
-
-        return 0
-
-    lax.fori_loop(0, n_blk * PIECES, drain, 0)
+    if cores > 1:
+        block_copy(tp, me, sibling, me, pair_send_sem.at[tp, me]).start()
     if n_sec > 1:
         for part in range(PARTS):
             w_copy(part).wait_send()
     for distance in range(1, n_blk):
         share_copy(distance).wait_send()
+    lax.fori_loop(0, peers, wait_block, 0)
+    if cores > 1:
+        lax.fori_loop(0, peers, wait_pair, 0)
+
+    def right_of(index):
+        right = blocks[index]
+        return jnp.concatenate(
+            [right[:, 0].reshape(width, width), right[:, 1].reshape(width, width)], axis=1
+        )
+
+    if dense:
+        lefts = [blocks[a, me].reshape(2 * quarter, width).astype(jnp.float32) for a in range(n_tp)]
+        sums = jnp.zeros((4 * quarter, 2 * width), jnp.float32)
+        for b in range(n_tp):
+            left = lefts[0] * counts[0][b]
+            for a in range(1, n_tp):
+                left = left + lefts[a] * counts[a][b]
+            high = left.astype(jnp.bfloat16)
+            low = (left - high.astype(jnp.float32)).astype(jnp.bfloat16)
+            sums = sums + jnp.dot(
+                jnp.concatenate([high, low], axis=0),
+                right_of(b),
+                preferred_element_type=jnp.float32,
+            )
+        sums = sums[: 2 * quarter] + sums[2 * quarter :]
+    else:
+        sums = jnp.zeros((2 * quarter, 2 * width), jnp.float32)
+        for g in range(slots):
+            active = jnp.where(g < loads[0], 1.0, 0.0)
+            left = blocks[diagrams[0, 0, g], me].reshape(2 * quarter, width)
+            left = (left.astype(jnp.float32) * active).astype(jnp.bfloat16)
+            sums = sums + jnp.dot(
+                left, right_of(diagrams[0, 1, g]), preferred_element_type=jnp.float32
+            )
+    scale = (width * slots) ** (-0.5)
+    out[0, 0, 0] = (sums[:quarter, :width] - sums[quarter:, width:]) * scale
+    out[0, 0, 1] = (sums[:quarter, width:] + sums[quarter:, :width]) * scale
+
 
     def drain_block(k, _):
-        copy, other = block_copy(k, True)
-
-        @pl.when(other)
+        copy, sent = own_block(k)
+
+        @pl.when(sent)
         def _():
             copy.wait_send()
+
+        if cores > 1:
+            pair_copy, passed = sibling_block(k)
+
+            @pl.when(passed)
+            def _():
+                pair_copy.wait_send()
 
         return 0
 
@@ -368,9 +452,10 @@
             dma((n_blk,)),
             dma((n_tp, n_blk)),
             dma((n_tp, n_blk)),
+            dma((n_tp, n_blk)),
         ],
         compiler_params=pltpu.CompilerParams(
-            collective_id=0, has_side_effects=True, vmem_limit_bytes=40 * 1024 * 1024
+            collective_id=0, has_side_effects=True, vmem_limit_bytes=60 * 1024 * 1024
         ),
     )(perambulator, backward, elementals, jnp.swapaxes(diagrams, 1, 2), owner_loads)
 

time: 50.6 us -> 45.8 us (0.905)
  local copies, waits for them, and re-layouts: 6.61 us -> 1.38 us
    unnamed x9 -> x1, local copies, waits for them, and re-layouts: 6.61 us -> 1.38 us
where the time goes in v3:
time: 45.8 us; the launch traced here: 45.2 us
  Pallas kernels  43.1 us (94%)
  local copies, waits for them, and re-layouts  1.38 us (3%)
  between operations  0.66 us (1%)
    pallas_call x1, Pallas kernels, on_device(): pl.pallas_call(functools.partial(kernel, n_sec, n_tp, n_blk), out_shape=j...  43.1 us
    unnamed x1, local copies, waits for them, and re-layouts  1.38 us

profile of v3, /device:TPU:0, one launch (start us, length us, event | category | flops | bytes accessed | tf_op | source)
XLA Modules:
  0.0 45.2 jit_solution(255806198841883039)
XLA Ops:
  0.7 43.1 %shard_map.55 = f32[1,1,2,32,128]{4,3,2,1,0:T(8,128)} custom-call(bf16[1,2,512,2048]{3,2,1,0:T(8,128)(2,1)} %tau_hbm.1, bf16[1,2,2048,512]{3,2,1,0:T(8,128)(2,1)} %beta_hbm.1, bf16[1,1,2,512,128]{4,3,2,1,0:T(8,128)(2,1)} %tile_hbm.1, s32[1,2,16]{2,1,0:T(2,128)} %bitcast.1, s32[1]{0:T(128)S(6)} %copy.7.loads), custom_call_target="tpu_custom_call" | custom-call | tf_op jit(solution)/shard_map/pallas_call | solution.py:427
  43.8 1.4 %copy.8 = f32[1,1,2,32,128]{4,3,2,1,0:T(8,128)} copy(f32[1,1,2,32,128]{4,3,2,1,0:T(8,128)} %shard_map.55) | data formatting | bytes 65536

commit v4 on v3

--- a/solution.py
+++ b/solution.py
@@ -150,20 +150,12 @@
         for r in range(PIECES):
             pass_on(upward, 0, part, r).start()
 
-    @pl.when(me < n_blk - 1)
-    def _():
-        send_own(1, 0)
-
-    @pl.when(me > 0)
-    def _():
-        send_own(0, 0)
-
-    for part in range(1, PARTS):
-        @pl.when(me == 0)
+    for part in range(PARTS):
+        @pl.when(me < n_blk - 1)
         def _():
             send_own(1, part)
 
-        @pl.when(me == n_blk - 1)
+        @pl.when(me > 0)
         def _():
             send_own(0, part)
 
@@ -191,12 +183,6 @@
                 @pl.when(more)
                 def _():
                     pass_on(below, distance, part, r).start()
-                    if part + 1 < PARTS:
-                        last = jnp.where(below == 1, chunk == 0, chunk == n_blk - 1)
-
-                        @pl.when(jnp.logical_and(last, r == PIECES - 1))
-                        def _():
-                            send_own(below, part + 1)
 
         def step(u, _):
             t, r = lax.div(u, PIECES), lax.rem(u, PIECES)
@@ -252,30 +238,106 @@
         lane < half, pltpu.roll(first, half, 1), second
     ).astype(jnp.bfloat16)
 
-    for part in range(PARTS):
+    share = half // n_blk
+
+    def share_copy(part, distance):
+        target = lax.rem(me + distance, n_blk)
+        where = pl.ds(pl.multiple_of(target * share, share), share)
+        return pltpu.make_async_remote_copy(
+            src_ref=partial.at[part, :, where, :],
+            dst_ref=shares.at[part, distance - 1],
+            send_sem=share_send_sem.at[part, distance - 1],
+            recv_sem=share_recv_sem.at[part, distance - 1],
+            device_id=(sec, tp, target),
+            device_id_type=MESH,
+        )
+
+    def block_copy(part, from_tp, from_blk, to_tp, to_blk, sem):
+        slot = blocks.at[from_tp, part * n_blk + from_blk]
+        return pltpu.make_async_remote_copy(
+            src_ref=slot,
+            dst_ref=slot,
+            send_sem=sem,
+            recv_sem=block_recv_sem.at[part, from_tp, from_blk],
+            device_id=(sec, to_tp, to_blk),
+            device_id_type=MESH,
+        )
+
+    def own_block(part, k):
+        other_tp, other_blk = lax.div(k, n_blk), lax.rem(k, n_blk)
+        sem = block_send_sem.at[part, other_tp, other_blk]
+        copy = block_copy(part, tp, me, other_tp, other_blk, sem)
+        return copy, same_core(other_tp, other_blk)
+
+    def sibling_block(part, k):
+        from_tp, from_blk = lax.div(k, n_blk), lax.rem(k, n_blk)
+        sem = pair_send_sem.at[part, from_tp, from_blk]
+        copy = block_copy(part, from_tp, from_blk, sibling, me, sem)
+        return copy, lax.rem(from_tp, cores) == core
+
+    def start_sum(part):
         if n_sec > 1:
             w_copy(part).wait_recv()
         product = jnp.dot(w_recv[part], image_full[...], preferred_element_type=jnp.float32)
-        own = pl.ds(part * half, half)
-        partial[0, own, :] = (product[:half, :width] + product[half:, width:]).astype(jnp.bfloat16)
-        partial[1, own, :] = (product[:half, width:] - product[half:, :width]).astype(jnp.bfloat16)
-
-    def rows_share(q):
-        return partial.at[:, pl.ds(pl.multiple_of(q * quarter, quarter), quarter), :]
-
-    def share_copy(distance):
-        target = lax.rem(me + distance, n_blk)
-        return pltpu.make_async_remote_copy(
-            src_ref=rows_share(target),
-            dst_ref=shares.at[distance - 1],
-            send_sem=share_send_sem.at[distance - 1],
-            recv_sem=share_recv_sem.at[distance - 1],
-            device_id=(sec, tp, target),
-            device_id_type=MESH,
-        )
-
-    for distance in range(1, n_blk):
-        share_copy(distance).start()
+        partial[part, 0] = (product[:half, :width] + product[half:, width:]).astype(jnp.bfloat16)
+        partial[part, 1] = (product[:half, width:] - product[half:, :width]).astype(jnp.bfloat16)
+        for distance in range(1, n_blk):
+            share_copy(part, distance).start()
+
+    def end_sum(part):
+        where = pl.ds(pl.multiple_of(me * share, share), share)
+        total = partial[part, :, where, :].astype(jnp.float32)
+        for distance in range(1, n_blk):
+            share_copy(part, distance).wait_recv()
+            total = total + shares[part, distance - 1].astype(jnp.float32)
+        blocks[tp, part * n_blk + me] = (total * order ** (-0.5)).astype(jnp.bfloat16)
+
+        def start_block(k, _):
+            copy, wanted = own_block(part, k)
+
+            @pl.when(wanted)
+            def _():
+                copy.start()
+
+            return 0
+
+        lax.fori_loop(0, peers, start_block, 0)
+        if cores > 1:
+            block_copy(part, tp, me, sibling, me, pair_send_sem.at[part, tp, me]).start()
+
+    def end_gather(part):
+        def wait_block(k, _):
+            other_tp, other_blk = lax.div(k, n_blk), lax.rem(k, n_blk)
+
+            @pl.when(same_core(other_tp, other_blk))
+            def _():
+                sem = block_send_sem.at[part, other_tp, other_blk]
+                block_copy(part, other_tp, other_blk, tp, me, sem).wait_recv()
+                if cores > 1:
+                    sibling_block(part, k)[0].start()
+
+            return 0
+
+        lax.fori_loop(0, peers, wait_block, 0)
+
+    def end_pair(part):
+        def wait_pair(k, _):
+            copy, passed = sibling_block(part, k)
+
+            @pl.when(jnp.logical_not(passed))
+            def _():
+                copy.wait_recv()
+
+            return 0
+
+        if cores > 1:
+            lax.fori_loop(0, peers, wait_pair, 0)
+
+    start_sum(0)
+    for part in range(PARTS):
+        end_sum(part)
+        if part + 1 < PARTS:
+            start_sum(part + 1)
 
     def drain(u, _):
         distance = lax.div(u, PIECES)
@@ -292,75 +354,16 @@
         return 0
 
     lax.fori_loop(0, n_blk * PIECES, drain, 0)
-    total = partial[:, pl.ds(pl.multiple_of(me * quarter, quarter), quarter), :].astype(jnp.float32)
-    for distance in range(1, n_blk):
-        share_copy(distance).wait_recv()
-        total = total + shares[distance - 1].astype(jnp.float32)
-    blocks[tp, me] = (total * order ** (-0.5)).astype(jnp.bfloat16)
-
-    def block_copy(from_tp, from_blk, to_tp, to_blk, sem):
-        slot = blocks.at[from_tp, from_blk]
-        return pltpu.make_async_remote_copy(
-            src_ref=slot,
-            dst_ref=slot,
-            send_sem=sem,
-            recv_sem=block_recv_sem.at[from_tp, from_blk],
-            device_id=(sec, to_tp, to_blk),
-            device_id_type=MESH,
-        )
-
-    def own_block(k):
-        other_tp, other_blk = lax.div(k, n_blk), lax.rem(k, n_blk)
-        copy = block_copy(tp, me, other_tp, other_blk, block_send_sem.at[other_tp, other_blk])
-        return copy, same_core(other_tp, other_blk)
-
-    def sibling_block(k):
-        from_tp, from_blk = lax.div(k, n_blk), lax.rem(k, n_blk)
-        copy = block_copy(from_tp, from_blk, sibling, me, pair_send_sem.at[from_tp, from_blk])
-        return copy, lax.rem(from_tp, cores) == core
-
-    def start_block(k, _):
-        copy, wanted = own_block(k)
-
-        @pl.when(wanted)
-        def _():
-            copy.start()
-
-        return 0
-
-    def wait_block(k, _):
-        other_tp, other_blk = lax.div(k, n_blk), lax.rem(k, n_blk)
-
-        @pl.when(same_core(other_tp, other_blk))
-        def _():
-            block_copy(
-                other_tp, other_blk, tp, me, block_send_sem.at[other_tp, other_blk]
-            ).wait_recv()
-            if cores > 1:
-                sibling_block(k)[0].start()
-
-        return 0
-
-    def wait_pair(k, _):
-        copy, passed = sibling_block(k)
-
-        @pl.when(jnp.logical_not(passed))
-        def _():
-            copy.wait_recv()
-
-        return 0
-
-    lax.fori_loop(0, peers, start_block, 0)
-    if cores > 1:
-        block_copy(tp, me, sibling, me, pair_send_sem.at[tp, me]).start()
     if n_sec > 1:
         for part in range(PARTS):
             w_copy(part).wait_send()
-    for distance in range(1, n_blk):
-        share_copy(distance).wait_send()
-    lax.fori_loop(0, peers, wait_block, 0)
-    if cores > 1:
-        lax.fori_loop(0, peers, wait_pair, 0)
+    for part in range(PARTS):
+        for distance in range(1, n_blk):
+            share_copy(part, distance).wait_send()
+    for part in range(PARTS):
+        end_gather(part)
+    for part in range(PARTS):
+        end_pair(part)
 
     def right_of(index):
         right = blocks[index]
@@ -368,8 +371,14 @@
             [right[:, 0].reshape(width, width), right[:, 1].reshape(width, width)], axis=1
         )
 
+    def left_of(index):
+        left = blocks[index, pl.ds(pl.multiple_of(me * PARTS, PARTS), PARTS)].astype(jnp.float32)
+        return jnp.concatenate(
+            [left[:, 0].reshape(quarter, width), left[:, 1].reshape(quarter, width)], axis=0
+        )
+
     if dense:
-        lefts = [blocks[a, me].reshape(2 * quarter, width).astype(jnp.float32) for a in range(n_tp)]
+        lefts = [left_of(a) for a in range(n_tp)]
         sums = jnp.zeros((4 * quarter, 2 * width), jnp.float32)
         for b in range(n_tp):
             left = lefts[0] * counts[0][b]
@@ -387,8 +396,7 @@
         sums = jnp.zeros((2 * quarter, 2 * width), jnp.float32)
         for g in range(slots):
             active = jnp.where(g < loads[0], 1.0, 0.0)
-            left = blocks[diagrams[0, 0, g], me].reshape(2 * quarter, width)
-            left = (left.astype(jnp.float32) * active).astype(jnp.bfloat16)
+            left = (left_of(diagrams[0, 0, g]) * active).astype(jnp.bfloat16)
             sums = sums + jnp.dot(
                 left, right_of(diagrams[0, 1, g]), preferred_element_type=jnp.float32
             )
@@ -398,18 +406,19 @@
 
 
     def drain_block(k, _):
-        copy, sent = own_block(k)
-
-        @pl.when(sent)
-        def _():
-            copy.wait_send()
-
-        if cores > 1:
-            pair_copy, passed = sibling_block(k)
-
-            @pl.when(passed)
-            def _():
-                pair_copy.wait_send()
+        for part in range(PARTS):
+            copy, sent = own_block(part, k)
+
+            @pl.when(sent)
+            def _():
+                copy.wait_send()
+
+            if cores > 1:
+                pair_copy, passed = sibling_block(part, k)
+
+                @pl.when(passed)
+                def _():
+                    pair_copy.wait_send()
 
         return 0
 
@@ -439,20 +448,20 @@
             pltpu.VMEM((PARTS, 2 * half, rows), jnp.bfloat16),
             pltpu.VMEM((PARTS, 2 * half, rows), jnp.bfloat16),
             pltpu.VMEM((rows, 2 * width), jnp.bfloat16),
-            pltpu.VMEM((2, width, width), jnp.bfloat16),
-            pltpu.VMEM((n_blk, 2, quarter, width), jnp.bfloat16),
-            pltpu.VMEM((n_tp, n_blk, 2, quarter, width), jnp.bfloat16),
+            pltpu.VMEM((PARTS, 2, half, width), jnp.bfloat16),
+            pltpu.VMEM((PARTS, n_blk, 2, half // n_blk, width), jnp.bfloat16),
+            pltpu.VMEM((n_tp, PARTS * n_blk, 2, half // n_blk, width), jnp.bfloat16),
             dma((2, n_blk)),
             dma,
             dma((2, n_blk, PARTS, PIECES)),
             dma((2, n_blk, PARTS, PIECES)),
             dma((PARTS,)),
             dma((PARTS,)),
-            dma((n_blk,)),
-            dma((n_blk,)),
-            dma((n_tp, n_blk)),
-            dma((n_tp, n_blk)),
-            dma((n_tp, n_blk)),
+            dma((PARTS, n_blk)),
+            dma((PARTS, n_blk)),
+            dma((PARTS, n_tp, n_blk)),
+            dma((PARTS, n_tp, n_blk)),
+            dma((PARTS, n_tp, n_blk)),
         ],
         compiler_params=pltpu.CompilerParams(
             collective_id=0, has_side_effects=True, vmem_limit_bytes=60 * 1024 * 1024

time: 45.8 us -> 44.4 us (0.969)
  Pallas kernels: 43.1 us -> 41.7 us
    pallas_call x1, Pallas kernels: 43.1 us -> 41.7 us  [on_device(): pl.pallas_call(functools.partial(kernel, n_sec, n_tp, n_blk), out_shape=j...]
where the time goes in v4:
time: 44.4 us; the launch traced here: 43.8 us
  Pallas kernels  41.7 us (94%)
  local copies, waits for them, and re-layouts  1.38 us (3%)
  between operations  0.66 us (1%)
    pallas_call x1, Pallas kernels, on_device(): pl.pallas_call(functools.partial(kernel, n_sec, n_tp, n_blk), out_shape=j...  41.7 us
    unnamed x1, local copies, waits for them, and re-layouts  1.38 us

profile of v4, /device:TPU:0, one launch (start us, length us, event | category | flops | bytes accessed | tf_op | source)
XLA Modules:
  0.0 43.8 jit_solution(4385863615364327961)
XLA Ops:
  0.7 41.7 %shard_map.55 = f32[1,1,2,32,128]{4,3,2,1,0:T(8,128)} custom-call(bf16[1,2,512,2048]{3,2,1,0:T(8,128)(2,1)} %tau_hbm.1, bf16[1,2,2048,512]{3,2,1,0:T(8,128)(2,1)} %beta_hbm.1, bf16[1,1,2,512,128]{4,3,2,1,0:T(8,128)(2,1)} %tile_hbm.1, s32[1,2,16]{2,1,0:T(2,128)} %bitcast.1, s32[1]{0:T(128)S(6)} %copy.7.loads), custom_call_target="tpu_custom_call" | custom-call | tf_op jit(solution)/shard_map/pallas_call | solution.py:436
  42.4 1.4 %copy.8 = f32[1,1,2,32,128]{4,3,2,1,0:T(8,128)} copy(f32[1,1,2,32,128]{4,3,2,1,0:T(8,128)} %shard_map.55) | data formatting | bytes 65536

commit v5 on v4

--- a/solution.py
+++ b/solution.py
@@ -18,7 +18,7 @@
     tau, beta, tile, gathered, image, conj_w, w_send, w_recv, image_full,
     partial, shares, blocks,
     load_sem, tile_sem, send_sem, recv_sem, w_send_sem, w_recv_sem,
-    share_send_sem, share_recv_sem, block_send_sem, block_recv_sem, pair_send_sem,
+    share_send_sem, share_recv_sem, block_send_sem, block_recv_sem,
 ):
     sec, tp, me = lax.axis_index("sec"), lax.axis_index("tp"), lax.axis_index("blk")
     rows, order = tau_hbm.shape[2], tau_hbm.shape[3]
@@ -58,32 +58,27 @@
     barrier = pltpu.get_barrier_semaphore()
     peers = n_tp * n_blk
 
-    cores = 2 if n_tp % 2 == 0 else 1
-    core = lax.rem(tp, cores)
-    sibling = tp + 1 - 2 * core
-
-    def same_core(other_tp, other_blk):
-        other = jnp.logical_or(other_tp != tp, other_blk != me)
-        return jnp.logical_and(other, lax.rem(other_tp, cores) == core)
-
-    def greet(k, _):
-        other_tp, other_blk = lax.div(k, n_blk), lax.rem(k, n_blk)
-
-        @pl.when(same_core(other_tp, other_blk))
-        def _():
-            pl.semaphore_signal(
-                barrier, inc=1, device_id=(sec, other_tp, other_blk), device_id_type=MESH
-            )
-
-        return 0
-
-    lax.fori_loop(0, peers, greet, 0)
+    def each_peer(visit):
+        def at(k):
+            other_tp = lax.rem(tp + lax.div(k, n_blk), n_tp)
+            other_blk = lax.rem(me + lax.rem(k, n_blk), n_blk)
+            visit(other_tp, other_blk)
+
+        if peers <= 16:
+            for k in range(peers - 1, 0, -1):
+                at(jnp.int32(k))
+        else:
+            lax.fori_loop(1, peers, lambda k, _: (at(k), 0)[1], 0)
+
+    def greet(other_tp, other_blk):
+        pl.semaphore_signal(
+            barrier, inc=1, device_id=(sec, other_tp, other_blk), device_id_type=MESH
+        )
+
+    each_peer(greet)
     sec_next = lax.rem(sec + 1, n_sec)
     sec_back = lax.rem(sec + n_sec - 1, n_sec)
-    greeted = peers // cores - 1
-    if cores > 1:
-        pl.semaphore_signal(barrier, inc=1, device_id=(sec, sibling, me), device_id_type=MESH)
-        greeted += 1
+    greeted = peers - 1
     if n_sec > 1:
         pl.semaphore_signal(barrier, inc=1, device_id=(sec_next, tp, me), device_id_type=MESH)
         greeted += 1
@@ -246,34 +241,35 @@
         return pltpu.make_async_remote_copy(
             src_ref=partial.at[part, :, where, :],
             dst_ref=shares.at[part, distance - 1],
-            send_sem=share_send_sem.at[part, distance - 1],
-            recv_sem=share_recv_sem.at[part, distance - 1],
+            send_sem=share_send_sem.at[part],
+            recv_sem=share_recv_sem.at[part],
             device_id=(sec, tp, target),
             device_id_type=MESH,
         )
 
-    def block_copy(part, from_tp, from_blk, to_tp, to_blk, sem):
-        slot = blocks.at[from_tp, part * n_blk + from_blk]
+    def all_shares(part):
+        every = shares.at[part]
+        return pltpu.make_async_remote_copy(
+            src_ref=every,
+            dst_ref=every,
+            send_sem=share_send_sem.at[part],
+            recv_sem=share_recv_sem.at[part],
+            device_id=(sec, tp, me),
+            device_id_type=MESH,
+        )
+
+    def block_copy(part, slot, other_tp, other_blk):
         return pltpu.make_async_remote_copy(
             src_ref=slot,
             dst_ref=slot,
-            send_sem=sem,
-            recv_sem=block_recv_sem.at[part, from_tp, from_blk],
-            device_id=(sec, to_tp, to_blk),
-            device_id_type=MESH,
-        )
-
-    def own_block(part, k):
-        other_tp, other_blk = lax.div(k, n_blk), lax.rem(k, n_blk)
-        sem = block_send_sem.at[part, other_tp, other_blk]
-        copy = block_copy(part, tp, me, other_tp, other_blk, sem)
-        return copy, same_core(other_tp, other_blk)
-
-    def sibling_block(part, k):
-        from_tp, from_blk = lax.div(k, n_blk), lax.rem(k, n_blk)
-        sem = pair_send_sem.at[part, from_tp, from_blk]
-        copy = block_copy(part, from_tp, from_blk, sibling, me, sem)
-        return copy, lax.rem(from_tp, cores) == core
+            send_sem=block_send_sem.at[part],
+            recv_sem=block_recv_sem.at[part],
+            device_id=(sec, other_tp, other_blk),
+            device_id_type=MESH,
+        )
+
+    def all_blocks(part):
+        return block_copy(part, blocks.at[part, pl.ds(0, peers - 1)], tp, me)
 
     def start_sum(part):
         if n_sec > 1:
@@ -287,51 +283,12 @@
     def end_sum(part):
         where = pl.ds(pl.multiple_of(me * share, share), share)
         total = partial[part, :, where, :].astype(jnp.float32)
+        all_shares(part).wait_recv()
         for distance in range(1, n_blk):
-            share_copy(part, distance).wait_recv()
             total = total + shares[part, distance - 1].astype(jnp.float32)
-        blocks[tp, part * n_blk + me] = (total * order ** (-0.5)).astype(jnp.bfloat16)
-
-        def start_block(k, _):
-            copy, wanted = own_block(part, k)
-
-            @pl.when(wanted)
-            def _():
-                copy.start()
-
-            return 0
-
-        lax.fori_loop(0, peers, start_block, 0)
-        if cores > 1:
-            block_copy(part, tp, me, sibling, me, pair_send_sem.at[part, tp, me]).start()
-
-    def end_gather(part):
-        def wait_block(k, _):
-            other_tp, other_blk = lax.div(k, n_blk), lax.rem(k, n_blk)
-
-            @pl.when(same_core(other_tp, other_blk))
-            def _():
-                sem = block_send_sem.at[part, other_tp, other_blk]
-                block_copy(part, other_tp, other_blk, tp, me, sem).wait_recv()
-                if cores > 1:
-                    sibling_block(part, k)[0].start()
-
-            return 0
-
-        lax.fori_loop(0, peers, wait_block, 0)
-
-    def end_pair(part):
-        def wait_pair(k, _):
-            copy, passed = sibling_block(part, k)
-
-            @pl.when(jnp.logical_not(passed))
-            def _():
-                copy.wait_recv()
-
-            return 0
-
-        if cores > 1:
-            lax.fori_loop(0, peers, wait_pair, 0)
+        own = tp * n_blk + me
+        blocks[part, own] = (total * order ** (-0.5)).astype(jnp.bfloat16)
+        each_peer(lambda *other: block_copy(part, blocks.at[part, own], *other).start())
 
     start_sum(0)
     for part in range(PARTS):
@@ -358,21 +315,21 @@
         for part in range(PARTS):
             w_copy(part).wait_send()
     for part in range(PARTS):
-        for distance in range(1, n_blk):
-            share_copy(part, distance).wait_send()
-    for part in range(PARTS):
-        end_gather(part)
-    for part in range(PARTS):
-        end_pair(part)
+        all_shares(part).wait_send()
+    for part in range(PARTS):
+        all_blocks(part).wait_recv()
 
     def right_of(index):
-        right = blocks[index]
+        first = index * n_blk
+        right = blocks[:, pl.ds(first, n_blk)].reshape(PARTS * n_blk, 2, share, width)
         return jnp.concatenate(
             [right[:, 0].reshape(width, width), right[:, 1].reshape(width, width)], axis=1
         )
 
     def left_of(index):
-        left = blocks[index, pl.ds(pl.multiple_of(me * PARTS, PARTS), PARTS)].astype(jnp.float32)
+        first = me * PARTS
+        at = index * n_blk + lax.rem(first, n_blk)
+        left = blocks[lax.div(first, n_blk), pl.ds(at, PARTS)].astype(jnp.float32)
         return jnp.concatenate(
             [left[:, 0].reshape(quarter, width), left[:, 1].reshape(quarter, width)], axis=0
         )
@@ -405,24 +362,8 @@
     out[0, 0, 1] = (sums[:quarter, width:] + sums[quarter:, :width]) * scale
 
 
-    def drain_block(k, _):
-        for part in range(PARTS):
-            copy, sent = own_block(part, k)
-
-            @pl.when(sent)
-            def _():
-                copy.wait_send()
-
-            if cores > 1:
-                pair_copy, passed = sibling_block(part, k)
-
-                @pl.when(passed)
-                def _():
-                    pair_copy.wait_send()
-
-        return 0
-
-    lax.fori_loop(0, peers, drain_block, 0)
+    for part in range(PARTS):
+        all_blocks(part).wait_send()
 
 
 def on_device(n_sec, n_tp, n_blk, perambulator, backward, elementals, diagrams, owner_loads):
@@ -449,19 +390,18 @@
             pltpu.VMEM((PARTS, 2 * half, rows), jnp.bfloat16),
             pltpu.VMEM((rows, 2 * width), jnp.bfloat16),
             pltpu.VMEM((PARTS, 2, half, width), jnp.bfloat16),
-            pltpu.VMEM((PARTS, n_blk, 2, half // n_blk, width), jnp.bfloat16),
-            pltpu.VMEM((n_tp, PARTS * n_blk, 2, half // n_blk, width), jnp.bfloat16),
+            pltpu.VMEM((PARTS, n_blk - 1, 2, half // n_blk, width), jnp.bfloat16),
+            pltpu.VMEM((PARTS, n_tp * n_blk, 2, half // n_blk, width), jnp.bfloat16),
             dma((2, n_blk)),
             dma,
             dma((2, n_blk, PARTS, PIECES)),
             dma((2, n_blk, PARTS, PIECES)),
             dma((PARTS,)),
             dma((PARTS,)),
-            dma((PARTS, n_blk)),
-            dma((PARTS, n_blk)),
-            dma((PARTS, n_tp, n_blk)),
-            dma((PARTS, n_tp, n_blk)),
-            dma((PARTS, n_tp, n_blk)),
+            dma((PARTS,)),
+            dma((PARTS,)),
+            dma((PARTS,)),
+            dma((PARTS,)),
         ],
         compiler_params=pltpu.CompilerParams(
             collective_id=0, has_side_effects=True, vmem_limit_bytes=60 * 1024 * 1024

time: 44.4 us -> 44.3 us (level)
  no operation moved by 1% of the time
where the time goes in v5:
time: 44.3 us; the launch traced here: 44.1 us
  Pallas kernels  42 us (95%)
  local copies, waits for them, and re-layouts  1.38 us (3%)
  between operations  0.66 us (1%)
    pallas_call x1, Pallas kernels, on_device(): pl.pallas_call(functools.partial(kernel, n_sec, n_tp, n_blk), out_shape=j...  42 us
    unnamed x1, local copies, waits for them, and re-layouts  1.38 us

profile of v5, /device:TPU:0, one launch (start us, length us, event | category | flops | bytes accessed | tf_op | source)
XLA Modules:
  0.0 44.1 jit_solution(11405340409845398807)
XLA Ops:
  0.7 42.0 %shard_map.55 = f32[1,1,2,32,128]{4,3,2,1,0:T(8,128)} custom-call(bf16[1,2,512,2048]{3,2,1,0:T(8,128)(2,1)} %tau_hbm.1, bf16[1,2,2048,512]{3,2,1,0:T(8,128)(2,1)} %beta_hbm.1, bf16[1,1,2,512,128]{4,3,2,1,0:T(8,128)(2,1)} %tile_hbm.1, s32[1,2,16]{2,1,0:T(2,128)} %bitcast.1, s32[1]{0:T(128)S(6)} %copy.7.loads), custom_call_target="tpu_custom_call" | custom-call | tf_op jit(solution)/shard_map/pallas_call | solution.py:377
  42.7 1.4 %copy.8 = f32[1,1,2,32,128]{4,3,2,1,0:T(8,128)} copy(f32[1,1,2,32,128]{4,3,2,1,0:T(8,128)} %shard_map.55) | data formatting | bytes 65536

commit v6 on v5

--- a/solution.py
+++ b/solution.py
@@ -164,61 +164,55 @@
             device_id_type=MESH,
         )
 
-    piece_lane = lax.broadcasted_iota(jnp.int32, (piece, width), 1)
-    for part in range(PARTS):
-        def receive(u):
-            t, r = lax.div(u, PIECES), lax.rem(u, PIECES)
-            distance, below, chunk = at_step(t)
-
-            @pl.when(jnp.logical_and(t > 0, u < n_blk * PIECES))
+    for part in range(PARTS):
+        def receive(t):
+            distance, below, _ = at_step(t)
+
+            @pl.when(jnp.logical_and(t > 0, t < n_blk))
             def _():
-                arrival(below, distance, part, r).wait_recv()
                 more = jnp.where(below == 1, me < n_blk - 1, me > 0)
-
-                @pl.when(more)
-                def _():
-                    pass_on(below, distance, part, r).start()
-
-        def step(u, _):
-            t, r = lax.div(u, PIECES), lax.rem(u, PIECES)
-            chunk = at_step(t)[2]
-
+                for r in range(PIECES):
+                    arrival(below, distance, part, r).wait_recv()
+
+                    @pl.when(more)
+                    def _():
+                        pass_on(below, distance, part, r).start()
+
+        def step(t, _):
             @pl.when(both > 0)
             def _():
-                receive(u + 1)
+                receive(t + 1)
 
             if part == 0:
-                @pl.when(r == 0)
-                def _():
-                    for copy in load(t):
-                        copy.wait()
-
-            where = pl.ds(pl.multiple_of(chunk * rows + r * piece, piece), piece)
+                for copy in load(t):
+                    copy.wait()
+
+            where = rows_of(at_step(t)[2])
             straight = gathered[part, where, :]
-            wide = straight.astype(jnp.float32)
-            turned = pltpu.roll(wide, half, 1)
-            turned = jnp.where(piece_lane < half, -turned, turned)
-            crossed = turned.astype(jnp.bfloat16)
+            turned = pltpu.roll(straight.astype(jnp.float32), half, 1)
+            crossed = jnp.where(lane < half, -turned, turned).astype(jnp.bfloat16)
             image[part] += jnp.dot(
-                tau[0, :, where], straight, preferred_element_type=jnp.float32
-            ) + jnp.dot(tau[1, :, where], crossed, preferred_element_type=jnp.float32)
-            conj_w[part] += jnp.dot(
-                wide.T.astype(jnp.bfloat16),
-                beta[0, where, :],
-                preferred_element_type=jnp.float32,
-            ) + jnp.dot(
-                (-turned).T.astype(jnp.bfloat16),
-                beta[1, where, :],
+                jnp.concatenate([tau[0, :, where], tau[1, :, where]], axis=1),
+                jnp.concatenate([straight, crossed], axis=0),
                 preferred_element_type=jnp.float32,
             )
+            upright = straight.T
+            upright = jnp.concatenate(
+                [upright, jnp.concatenate([upright[half:], -upright[:half]], axis=0)], axis=1
+            )
+            conj_w[part] += jnp.dot(
+                upright,
+                jnp.concatenate([beta[0, where, :], beta[1, where, :]], axis=0),
+                preferred_element_type=jnp.float32,
+            )
 
             @pl.when(both == 0)
             def _():
-                receive(u + 1)
+                receive(t + 1)
 
             return 0
 
-        lax.fori_loop(0, n_blk * PIECES, step, 0)
+        lax.fori_loop(0, n_blk, step, 0)
         if n_sec > 1:
             w_send[part] = conj_w[part].astype(jnp.bfloat16)
             w_copy(part).start()

time: 44.3 us -> 44.4 us (level)
  no operation moved by 1% of the time
where the time goes in v6:
time: 44.4 us; the launch traced here: 44.2 us
  Pallas kernels  42.2 us (95%)
  local copies, waits for them, and re-layouts  1.38 us (3%)
  between operations  0.66 us (1%)
    pallas_call x1, Pallas kernels, on_device(): pl.pallas_call(functools.partial(kernel, n_sec, n_tp, n_blk), out_shape=j...  42.2 us
    unnamed x1, local copies, waits for them, and re-layouts  1.38 us

profile of v6, /device:TPU:0, one launch (start us, length us, event | category | flops | bytes accessed | tf_op | source)
XLA Modules:
  0.0 44.2 jit_solution(10386883399131436693)
XLA Ops:
  0.7 42.2 %shard_map.55 = f32[1,1,2,32,128]{4,3,2,1,0:T(8,128)} custom-call(bf16[1,2,512,2048]{3,2,1,0:T(8,128)(2,1)} %tau_hbm.1, bf16[1,2,2048,512]{3,2,1,0:T(8,128)(2,1)} %beta_hbm.1, bf16[1,1,2,512,128]{4,3,2,1,0:T(8,128)(2,1)} %tile_hbm.1, s32[1,2,16]{2,1,0:T(2,128)} %bitcast.1, s32[1]{0:T(128)S(6)} %copy.7.loads), custom_call_target="tpu_custom_call" | custom-call | tf_op jit(solution)/shard_map/pallas_call | solution.py:371
  42.9 1.4 %copy.8 = f32[1,1,2,32,128]{4,3,2,1,0:T(8,128)} copy(f32[1,1,2,32,128]{4,3,2,1,0:T(8,128)} %shard_map.55) | data formatting | bytes 65536

commit v7 on v5

--- a/solution.py
+++ b/solution.py
@@ -195,23 +195,32 @@
 
             where = pl.ds(pl.multiple_of(chunk * rows + r * piece, piece), piece)
             straight = gathered[part, where, :]
-            wide = straight.astype(jnp.float32)
-            turned = pltpu.roll(wide, half, 1)
-            turned = jnp.where(piece_lane < half, -turned, turned)
-            crossed = turned.astype(jnp.bfloat16)
-            image[part] += jnp.dot(
-                tau[0, :, where], straight, preferred_element_type=jnp.float32
-            ) + jnp.dot(tau[1, :, where], crossed, preferred_element_type=jnp.float32)
+            upright = straight.T
+            upright = jnp.concatenate(
+                [upright, jnp.concatenate([upright[half:], -upright[:half]], axis=0)], axis=1
+            )
             conj_w[part] += jnp.dot(
-                wide.T.astype(jnp.bfloat16),
-                beta[0, where, :],
-                preferred_element_type=jnp.float32,
-            ) + jnp.dot(
-                (-turned).T.astype(jnp.bfloat16),
-                beta[1, where, :],
+                upright,
+                jnp.concatenate([beta[0, where, :], beta[1, where, :]], axis=0),
                 preferred_element_type=jnp.float32,
             )
 
+            @pl.when(u == n_blk * PIECES - 1)
+            def _():
+                if n_sec > 1:
+                    w_send[part] = conj_w[part].astype(jnp.bfloat16)
+                    w_copy(part).start()
+                else:
+                    w_recv[part] = conj_w[part].astype(jnp.bfloat16)
+
+            turned = pltpu.roll(straight.astype(jnp.float32), half, 1)
+            crossed = jnp.where(piece_lane < half, -turned, turned).astype(jnp.bfloat16)
+            image[part] += jnp.dot(
+                jnp.concatenate([tau[0, :, where], tau[1, :, where]], axis=1),
+                jnp.concatenate([straight, crossed], axis=0),
+                preferred_element_type=jnp.float32,
+            )
+
             @pl.when(both == 0)
             def _():
                 receive(u + 1)
@@ -219,11 +228,6 @@
             return 0
 
         lax.fori_loop(0, n_blk * PIECES, step, 0)
-        if n_sec > 1:
-            w_send[part] = conj_w[part].astype(jnp.bfloat16)
-            w_copy(part).start()
-        else:
-            w_recv[part] = conj_w[part].astype(jnp.bfloat16)
 
     first, second = image[0], image[1]
     image_full[:, :width] = jnp.where(

time: 44.3 us -> 45.3 us (1.023)
  Pallas kernels: 42 us -> 43.1 us
    pallas_call x1, Pallas kernels: 42 us -> 43.1 us  [on_device(): pl.pallas_call(functools.partial(kernel, n_sec, n_tp, n_blk), out_shape=j...]
where the time goes in v7:
time: 45.3 us; the launch traced here: 45.1 us
  Pallas kernels  43.1 us (95%)
  local copies, waits for them, and re-layouts  1.38 us (3%)
  between operations  0.66 us (1%)
    pallas_call x1, Pallas kernels, on_device(): pl.pallas_call(functools.partial(kernel, n_sec, n_tp, n_blk), out_shape=j...  43.1 us
    unnamed x1, local copies, waits for them, and re-layouts  1.38 us

profile of v7, /device:TPU:0, one launch (start us, length us, event | category | flops | bytes accessed | tf_op | source)
XLA Modules:
  0.0 45.1 jit_solution(15425944106231637221)
XLA Ops:
  0.7 43.1 %shard_map.55 = f32[1,1,2,32,128]{4,3,2,1,0:T(8,128)} custom-call(bf16[1,2,512,2048]{3,2,1,0:T(8,128)(2,1)} %tau_hbm.1, bf16[1,2,2048,512]{3,2,1,0:T(8,128)(2,1)} %beta_hbm.1, bf16[1,1,2,512,128]{4,3,2,1,0:T(8,128)(2,1)} %tile_hbm.1, s32[1,2,16]{2,1,0:T(2,128)} %bitcast.1, s32[1]{0:T(128)S(6)} %copy.7.loads), custom_call_target="tpu_custom_call" | custom-call | tf_op jit(solution)/shard_map/pallas_call | solution.py:381
  43.8 1.4 %copy.8 = f32[1,1,2,32,128]{4,3,2,1,0:T(8,128)} copy(f32[1,1,2,32,128]{4,3,2,1,0:T(8,128)} %shard_map.55) | data formatting | bytes 65536

commit v8 on v5

--- a/solution.py
+++ b/solution.py
@@ -199,9 +199,6 @@
             turned = pltpu.roll(wide, half, 1)
             turned = jnp.where(piece_lane < half, -turned, turned)
             crossed = turned.astype(jnp.bfloat16)
-            image[part] += jnp.dot(
-                tau[0, :, where], straight, preferred_element_type=jnp.float32
-            ) + jnp.dot(tau[1, :, where], crossed, preferred_element_type=jnp.float32)
             conj_w[part] += jnp.dot(
                 wide.T.astype(jnp.bfloat16),
                 beta[0, where, :],
@@ -212,6 +209,18 @@
                 preferred_element_type=jnp.float32,
             )
 
+            @pl.when(u == n_blk * PIECES - 1)
+            def _():
+                if n_sec > 1:
+                    w_send[part] = conj_w[part].astype(jnp.bfloat16)
+                    w_copy(part).start()
+                else:
+                    w_recv[part] = conj_w[part].astype(jnp.bfloat16)
+
+            image[part] += jnp.dot(
+                tau[0, :, where], straight, preferred_element_type=jnp.float32
+            ) + jnp.dot(tau[1, :, where], crossed, preferred_element_type=jnp.float32)
+
             @pl.when(both == 0)
             def _():
                 receive(u + 1)
@@ -219,11 +228,6 @@
             return 0
 
         lax.fori_loop(0, n_blk * PIECES, step, 0)
-        if n_sec > 1:
-            w_send[part] = conj_w[part].astype(jnp.bfloat16)
-            w_copy(part).start()
-        else:
-            w_recv[part] = conj_w[part].astype(jnp.bfloat16)
 
     first, second = image[0], image[1]
     image_full[:, :width] = jnp.where(

time: 44.3 us -> 45.5 us (1.027)
  Pallas kernels: 42 us -> 43.3 us
    pallas_call x1, Pallas kernels: 42 us -> 43.3 us  [on_device(): pl.pallas_call(functools.partial(kernel, n_sec, n_tp, n_blk), out_shape=j...]
where the time goes in v8:
time: 45.5 us; the launch traced here: 45.3 us
  Pallas kernels  43.3 us (95%)
  local copies, waits for them, and re-layouts  1.38 us (3%)
  between operations  0.66 us (1%)
    pallas_call x1, Pallas kernels, on_device(): pl.pallas_call(functools.partial(kernel, n_sec, n_tp, n_blk), out_shape=j...  43.3 us
    unnamed x1, local copies, waits for them, and re-layouts  1.38 us

profile of v8, /device:TPU:0, one launch (start us, length us, event | category | flops | bytes accessed | tf_op | source)
XLA Modules:
  0.0 45.3 jit_solution(1865150082685673110)
XLA Ops:
  0.7 43.3 %shard_map.55 = f32[1,1,2,32,128]{4,3,2,1,0:T(8,128)} custom-call(bf16[1,2,512,2048]{3,2,1,0:T(8,128)(2,1)} %tau_hbm.1, bf16[1,2,2048,512]{3,2,1,0:T(8,128)(2,1)} %beta_hbm.1, bf16[1,1,2,512,128]{4,3,2,1,0:T(8,128)(2,1)} %tile_hbm.1, s32[1,2,16]{2,1,0:T(2,128)} %bitcast.1, s32[1]{0:T(128)S(6)} %copy.7.loads), custom_call_target="tpu_custom_call" | custom-call | tf_op jit(solution)/shard_map/pallas_call | solution.py:381
  43.9 1.4 %copy.8 = f32[1,1,2,32,128]{4,3,2,1,0:T(8,128)} copy(f32[1,1,2,32,128]{4,3,2,1,0:T(8,128)} %shard_map.55) | data formatting | bytes 65536
